TPU v7x, 128 devices: a whole 4x4x4 slice. The times are simulated.
128 devices in a mesh: row: 8 (over z_lo, x), col: 16 (over y, z_hi, core).
Axes of the slice: x: 4, y: 4, z: 4 (z_hi: 2, z_lo: 2; z = z_hi * 2 + z_lo), core: 2. Of those that a mesh axis runs over, the one named last changes fastest.
Arguments:
- eigenvectors: bfloat16 [28672, 28672], P('col', 'row'), may hold values from -0.75 to 0.75
- reflectors_first: bfloat16 [28672, 256], P(('row', 'col')), may hold values from -600 to 600, as said below
- reflectors_second: bfloat16 [28672, 256], P(('row', 'col')), may hold values from -600 to 600, as said below
- forget_gradient: bfloat16 [256, 28672], P(None, ('row', 'col')), may hold values from -0.03125 to 0.03125
Outputs:
- eigenvectors_new: bfloat16 [28672, 28672], P(('col', 'row'))
- rotated_gradient: bfloat16 [28672, 256], P(('col', 'row'))
Inputs may be any that keep to these rules, and one draw needn't show every extreme that they name: `reflectors_first`: the columns are the vectors of 256 Householder reflectors. `reflectors_second`: the columns are the vectors of 256 Householder reflectors.
All inputs are finite; a program needn't handle non-finite values.
Results may differ from a plain program's by a relative error of at most 0.0051.
Values may be sent and summed in bfloat16 or wider, within the bound.
A program may use at most 128 MiB of HBM per device.

v0:
```python
import jax
import jax.numpy as jnp
from jax import lax
from jax.sharding import PartitionSpec as P


def inner_products(left_side, right_side):
    return lax.dot_general(
        left_side, right_side, (((0,), (0,)), ((), ())), preferred_element_type=jnp.float32
    )


def upper_factor(gram_block):
    return jnp.triu(gram_block) - 0.5 * jnp.diag(jnp.diag(gram_block))


def upper_inverse(gram_block):
    factor = upper_factor(gram_block)
    order = factor.shape[0]
    identity = jnp.eye(order, dtype=factor.dtype)

    def backward_row(counter, inverse_rows):
        index = (order - 1 - counter).astype(jnp.int32)
        factor_row = lax.dynamic_slice_in_dim(factor, index, 1, 0)
        unit_row = lax.dynamic_slice_in_dim(identity, index, 1, 0)
        pivot_entry = lax.dynamic_slice(factor, (index, index), (1, 1))
        filled = jnp.dot(
            factor_row,
            inverse_rows,
            precision=lax.Precision.HIGHEST,
            preferred_element_type=factor.dtype,
        )
        fresh_row = (unit_row - filled) / pivot_entry
        return lax.dynamic_update_slice_in_dim(inverse_rows, fresh_row, index, 0)

    return lax.fori_loop(0, order, backward_row, jnp.zeros_like(factor))


def solve_coefficients(products, gram_first, gram_second, cross_gram, block_width):
    inverse_first = upper_inverse(gram_first)
    inverse_second = upper_inverse(gram_second)
    coef_first = jnp.dot(
        products[:, :block_width],
        inverse_first,
        precision=lax.Precision.HIGHEST,
        preferred_element_type=jnp.float32,
    )
    shifted = products[:, block_width:] - jnp.dot(
        coef_first, cross_gram, precision=lax.Precision.HIGHEST, preferred_element_type=jnp.float32
    )
    coef_second = jnp.dot(
        shifted, inverse_second, precision=lax.Precision.HIGHEST, preferred_element_type=jnp.float32
    )
    return jnp.concatenate([coef_first, coef_second], axis=1).astype(jnp.bfloat16)


def body(eigenvectors, reflectors_first, reflectors_second, forget_gradient):
    block_width = reflectors_first.shape[1]
    own_sets = jnp.concatenate([reflectors_first, reflectors_second], axis=1)
    both_sets = lax.all_gather(own_sets, "col", axis=0, tiled=True)
    set_first = both_sets[:, :block_width]
    set_second = both_sets[:, block_width:]
    gram_first = inner_products(set_first, set_first)
    gram_second = inner_products(set_second, set_second)
    cross_gram = inner_products(set_first, set_second)
    products = jnp.dot(eigenvectors, both_sets, preferred_element_type=jnp.float32)
    products, gram_first, gram_second, cross_gram = lax.psum(
        (products, gram_first, gram_second, cross_gram), "row"
    )
    coefficients = solve_coefficients(products, gram_first, gram_second, cross_gram, block_width)
    update = lax.dot_general(
        coefficients, both_sets, (((1,), (1,)), ((), ())), preferred_element_type=jnp.float32
    )
    renewed = (eigenvectors.astype(jnp.float32) - update).astype(jnp.bfloat16)
    eig_slab = lax.all_to_all(renewed, "row", split_axis=0, concat_axis=1, tiled=True)
    rotated = lax.dot_general(
        eig_slab,
        lax.all_gather(forget_gradient, ("row", "col"), axis=1, tiled=True),
        (((1,), (1,)), ((), ())),
        preferred_element_type=jnp.float32,
    )
    return (eig_slab, rotated.astype(jnp.bfloat16))


def solution(mesh):
    return jax.shard_map(
        body,
        mesh=mesh,
        in_specs=(
            P("col", "row"),
            P(("row", "col"), None),
            P(("row", "col"), None),
            P(None, ("row", "col")),
        ),
        out_specs=(P(("col", "row"), None), P(("col", "row"), None)),
        check_vma=False,
    )
```

profile of v0, /device:TPU:0, one launch (start us, length us, event | category | flops | bytes accessed | tf_op | source)
XLA Modules:
  0.0 1186.7 jit_solution(10317816178154016701)
XLA Ops:
  8.0 1.7 pad_maximum_fusion
  9.8 58.8 %all-gather.3.cloned.1.call-done = bf16[3584,512]{1,0:T(8,128)(2,1)} async-done(((bf16[224,512]{1,0:T(8,128)(2,1)}), bf16[3584,512]{1,0:T(8,128)(2,1)}) %all-gather.3.cloned.1.call-update) | async-done | bytes 3670032 | tf_op jit(solution)/shard_map/all_gather | solution.py:60
  68.6 3.6 fusion.13
  72.1 1.4 fusion.15
  73.5 1.4 fusion.18
  74.9 11.8 convolution_bitcast_fusion
  87.3 122.9 %all-reduce.3.cloned.1.call-done = (f32[256,256]{1,0:T(8,128)}, f32[1792,512]{0,1:T(8,128)}, f32[256,256]{1,0:T(8,128)}, f32[256,256]{1,0:T(8,128)}) async-done(((f32[256,256]{1,0:T(8,128)}, f32[1792,512]{0,1:T(8,128)}, f32[256,256]{1,0:T(8,128)}, f32[256,256]{1,0:T(8,128)}), (f32[256,256]{1,0:T(8,128)}, f32[1792,512]{0,1:T(8,128)}, f32[256,256]{1,0:T(8,128)}, ...) | async-done | bytes 4456464 | tf_op jit(solution)/shard_map/psum | solution.py:67
  210.3 2.6 gather_fusion
  212.8 2.6 gather_fusion.1
  215.4 1.2 multiply_subtract_fusion
  216.6 387.5 %while.30 = (s32[]{:T(128)}, f32[256,256]{1,0:T(8,128)S(1)}, f32[256,256]{1,0:T(8,128)S(1)}, f32[256,256]{1,0:T(8,128)S(1)}, s32[]{:T(128)}, /*index=5*/s32[]{:T(128)}, s32[]{:T(128)}, s32[]{:T(128)}) while((s32[]{:T(128)}, f32[256,256]{1,0:T(8,128)S(1)}, f32[256,256]{1,0:T(8,128)S(1)}, f32[256,256]{1,0:T(8,128)S(1)}, s32[]{:T(128)}, ...), condition=%wide.region_3.0_spmd, body=%wide.region_2.0_spmd.sunk | while | flops 786950 | bytes 268439 | solution.py:36
  258.1 0.9 fusion.43
  280.8 0.8 fusion.43
  308.1 0.9 fusion.43
  335.3 0.8 fusion.43
  361.1 0.8 fusion.43
  604.2 387.5 %while.31 = (s32[]{:T(128)}, f32[256,256]{1,0:T(8,128)S(1)}, f32[256,256]{1,0:T(8,128)S(1)}, f32[256,256]{1,0:T(8,128)S(1)}, s32[]{:T(128)}, /*index=5*/s32[]{:T(128)}, s32[]{:T(128)}, s32[]{:T(128)}) while((s32[]{:T(128)}, f32[256,256]{1,0:T(8,128)S(1)}, f32[256,256]{1,0:T(8,128)S(1)}, f32[256,256]{1,0:T(8,128)S(1)}, s32[]{:T(128)}, ...), condition=%wide.region_7.8_spmd, body=%wide.region_6.7_spmd.sunk | while | flops 786950 | bytes 268439 | solution.py:36
  991.8 3.4 fusion.22
  995.2 1.9 convolution_subtract_fusion.2
  997.1 1.8 convolution_convert_fusion
  998.9 13.9 %subtract_convert_fusion = bf16[1792,3584]{1,0:T(8,128)(2,1)} fusion(bf16[1792,3584]{1,0:T(8,128)(2,1)} %param.8, bf16[3584,512]{1,0:T(8,128)(2,1)} %all-gather.3.cloned.1.call-done, bf16[1792,256]{0,1:T(8,128)(2,1)S(1)} %convolution_convert_fusion, bf16[1792,256]{0,1:T(8,128)(2,1)S(1)} %get-tuple-element.246), kind=kOutput, calls=%fused_computation.12 | convolution fusion | flops 6599606272 | bytes 31195136 | tf_op jit(solution)/shard_map/dot_general | solution.py:71
  1012.8 148.0 %all_to_all.19 = bf16[8,224,3584]{2,1,0:T(8,128)(2,1)S(1)} all-to-all(bf16[8,224,3584]{2,1,0:T(8,128)(2,1)} %bitcast.48), channel_id=1, replica_groups=mesh['row'=8,'col'=16] {'row'}, dimensions={0} | all-to-all | bytes 25690112 | tf_op jit(solution)/shard_map/all_to_all | solution.py:75
  1160.8 5.5 copy.8
  1166.3 12.9 %convolution_convert_fusion.1 = bf16[224,256]{1,0:T(8,128)(2,1)} fusion(bf16[224,28672]{1,0:T(8,128)(2,1)} %bitcast.46, bf16[256,28672]{0,1:T(8,128)(2,1)} %all-gather.5.cloned.1.call-done), kind=kOutput, calls=%fused_computation.28 | convolution fusion | flops 3288391680 | bytes 27639808 | tf_op jit(solution)/shard_map/dot_general | solution.py:76
  (1549 shorter events, 757.3 us)
Async XLA Ops:
  8.0 60.6 %all-gather.3.cloned.1.call-start = ((), (), s32[]{:S(2)}) async-start(), calls=%async_computation.1 | async-start | bytes 3899392 | tf_op jit(solution)/shard_map/all_gather | solution.py:60
  9.7 200.5 %all-reduce.3.cloned.1.call-start = ((), (), s32[]{:S(2)}) async-start(), calls=%async_computation.3 | async-start | bytes 8912896 | tf_op jit(solution)/shard_map/psum | solution.py:67
  68.5 3.6 copy-start.2
  86.7 1079.6 %all-gather.5.cloned.1.call-start = ((), (), s32[]{:S(2)}) async-start(), calls=%async_computation.2 | async-start | bytes 14794752 | tf_op jit(solution)/shard_map/all_gather | solution.py:78
  604.2 391.0 %copy-start.1 = (f32[256,256]{1,0:T(8,128)S(1)}, f32[256,256]{1,0:T(8,128)}, u32[]{:S(2)}) copy-start(f32[256,256]{1,0:T(8,128)} %get-tuple-element.242) | copy-start | bytes 786436
  991.7 3.5 copy-start
Sparse Core Ops, SparseCore 0:
  11.8 56.6 all-gather.2
  86.8 123.3 all-reduce.2
Sparse Core Ops, SparseCore 1:
  88.9 285.2 all-gather.4
where the time goes:
time: 1210 us; the launch traced here: 1190 us
  matrix products  477 us (39%)
  local copies, waits for them, and re-layouts  346 us (29%)
  waiting for transfers between devices  182 us (15%)
  blocking collectives  148 us (12%)
  between operations  15.6 us (1%)
  loops' own time  14.3 us (1%)
    dot_general x512, matrix products, backward_row(): jnp.dot(factor_row, inverse_rows, precision=lax.Precision.HIGHEST, prefer...  425 us
    dynamic_slice x512, local copies, waits for them, and re-layouts, backward_row(): pivot_entry = lax.dynamic_slice(factor, (index, index), (1, 1))  302 us
    all_to_all x1, blocking collectives, body(): lax.all_to_all(renewed, 'row', split_axis=0, concat_axis=1, tiled=True)  148 us
    psum x1, waiting for transfers between devices, body(): lax.psum((products, gram_first, gram_second, cross_gram), 'row')  123 us
    all_gather x1, waiting for transfers between devices, body(): both_sets = lax.all_gather(own_sets, 'col', axis=0, tiled=True)  58.8 us
    dynamic_update_slice x512, local copies, waits for them, and re-layouts, backward_row(): return lax.dynamic_update_slice_in_dim(inverse_rows, fresh_row, index, 0)  33.3 us
  transfers between devices with their start and end apart: 3, of which 2 were waited for; matrix products, arithmetic and copies ran while one was open for 67% of the time, Pallas kernels for 0%

commit v1 on v0

v1 whole, which is shorter than its diff:
```python
import jax
import jax.numpy as jnp
from jax import lax
from jax.experimental import pallas as pl
from jax.experimental.pallas import tpu as pltpu
from jax.sharding import PartitionSpec as P

HIGH = lax.Precision.HIGHEST


def inner_products(left_side, right_side):
    return lax.dot_general(
        left_side, right_side, (((0,), (0,)), ((), ())), preferred_element_type=jnp.float32
    )


def exact(left_side, right_side):
    return jnp.dot(left_side, right_side, precision=HIGH, preferred_element_type=jnp.float32)


def inverse_kernel(gram_ref, inverse_ref):
    order = gram_ref.shape[0]
    half = order // 2
    gram = gram_ref[...]
    rows = lax.broadcasted_iota(jnp.int32, (half, half), 0)
    cols = lax.broadcasted_iota(jnp.int32, (half, half), 1)
    parts = [gram[:half, :half], gram[half:, half:]]
    inverses = [jnp.where(rows == cols, 2.0 / part, 0.0) for part in parts]
    for level in range(half.bit_length() - 1):
        row_block, col_block = lax.shift_right_logical(rows, level), lax.shift_right_logical(cols, level)
        corner = (row_block + 1 == col_block) & ((row_block & 1) == 0)
        corners = [jnp.where(corner, part, 0.0) for part in parts]
        steps = [exact(c, i) for c, i in zip(corners, inverses)]
        inverses = [i - exact(i, s) for i, s in zip(inverses, steps)]
    cross = exact(inverses[0], exact(gram[:half, half:], inverses[1]))
    inverse_ref[:half, :half] = inverses[0]
    inverse_ref[half:, half:] = inverses[1]
    inverse_ref[:half, half:] = -cross
    inverse_ref[half:, :half] = jnp.zeros((half, half), jnp.float32)


def block_inverse(gram):
    return pl.pallas_call(
        inverse_kernel,
        out_shape=jax.ShapeDtypeStruct(gram.shape, jnp.float32),
        in_specs=[pl.BlockSpec(memory_space=pltpu.VMEM)],
        out_specs=pl.BlockSpec(memory_space=pltpu.VMEM),
        compiler_params=pltpu.CompilerParams(vmem_limit_bytes=32 * 1024 * 1024),
        name="block_inverse",
    )(gram)


def body(eigenvectors, reflectors_first, reflectors_second, forget_gradient):
    own_sets = jnp.concatenate([reflectors_first, reflectors_second], axis=1)
    both_sets = lax.all_gather(own_sets, "col", axis=0, tiled=True)
    gram = lax.psum(inner_products(both_sets, both_sets), "row")
    products = jnp.dot(eigenvectors, both_sets, preferred_element_type=jnp.float32)
    products = lax.psum(products, "row")
    coefficients = exact(products, block_inverse(gram)).astype(jnp.bfloat16)
    update = lax.dot_general(
        coefficients, both_sets, (((1,), (1,)), ((), ())), preferred_element_type=jnp.float32
    )
    renewed = (eigenvectors.astype(jnp.float32) - update).astype(jnp.bfloat16)
    eig_slab = lax.all_to_all(renewed, "row", split_axis=0, concat_axis=1, tiled=True)
    rotated = lax.dot_general(
        eig_slab,
        lax.all_gather(forget_gradient, ("row", "col"), axis=1, tiled=True),
        (((1,), (1,)), ((), ())),
        preferred_element_type=jnp.float32,
    )
    return (eig_slab, rotated.astype(jnp.bfloat16))


def solution(mesh):
    return jax.shard_map(
        body,
        mesh=mesh,
        in_specs=(
            P("col", "row"),
            P(("row", "col"), None),
            P(("row", "col"), None),
            P(None, ("row", "col")),
        ),
        out_specs=(P(("col", "row"), None), P(("col", "row"), None)),
        check_vma=False,
    )
```

time: 1210 us -> 490 us (0.40); the launches traced: 1190 us -> 489 us
  matrix products: 477 us -> 51.9 us
  local copies, waits for them, and re-layouts: 346 us -> 6.75 us
  waiting for transfers between devices: 182 us -> 221 us
  blocking collectives: 148 us -> 181 us
  loops' own time: 14.3 us -> 0 us
    dot_general x515 -> x1, matrix products: 432 us -> 8.03 us  [exact(): jnp.dot(left_side, right_side, precision=HIGH, preferred_element_type=jnp...]
    dynamic_slice x512 -> x0, local copies, waits for them, and re-layouts: 302 us -> none  [backward_row(): pivot_entry = lax.dynamic_slice(factor, (index, index), (1, 1))]
    all_gather x1, waiting for transfers between devices: 0.01 us -> 35.9 us  [body(): lax.all_gather(forget_gradient, ('row', 'col'), axis=1, tiled=True)]
    dynamic_update_slice x512 -> x0, local copies, waits for them, and re-layouts: 33.3 us -> none  [backward_row(): return lax.dynamic_update_slice_in_dim(inverse_rows, fresh_row, index, 0)]
    all_to_all x1, blocking collectives: 148 us -> 181 us  [body(): lax.all_to_all(renewed, 'row', split_axis=0, concat_axis=1, tiled=True)]
    another operation x2 -> x0, loops' own time: 14.3 us -> none  [upper_inverse(): return lax.fori_loop(0, order, backward_row, jnp.zeros_like(factor))]
  transfers between devices with their start and end apart: 3 -> 3, of which waited for: 2 -> 3; matrix products, arithmetic and copies ran while one was open for 67% -> 5% of each run, Pallas kernels for 0% -> 2%
where the time goes in v1:
time: 490 us; the launch traced here: 489 us
  waiting for transfers between devices  221 us (45%)
  blocking collectives  181 us (37%)
  matrix products  51.9 us (11%)
  between operations  15.5 us (3%)
  Pallas kernels  10.7 us (2%)
  local copies, waits for them, and re-layouts  6.75 us (1%)
    all_to_all x1, blocking collectives, body(): lax.all_to_all(renewed, 'row', split_axis=0, concat_axis=1, tiled=True)  181 us
    psum x1, waiting for transfers between devices, body(): products = lax.psum(products, 'row')  126 us
    all_gather x1, waiting for transfers between devices, body(): both_sets = lax.all_gather(own_sets, 'col', axis=0, tiled=True)  58.8 us
    all_gather x1, waiting for transfers between devices, body(): lax.all_gather(forget_gradient, ('row', 'col'), axis=1, tiled=True)  35.9 us
    dot_general x1, matrix products, body(): lax.dot_general(eig_slab, lax.all_gather(forget_gradient, ('row', 'col'),...  12.9 us
    dot_general x1, matrix products, body(): lax.dot_general(coefficients, both_sets, (((1,), (1,)), ((), ())), prefer...  12.7 us
    dot_general x1, matrix products, body(): jnp.dot(eigenvectors, both_sets, preferred_element_type=jnp.float32)  11.8 us
    pallas_call x1, Pallas kernels, block_inverse(): pl.pallas_call(inverse_kernel, out_shape=jax.ShapeDtypeStruct(gram.shape,...  10.7 us
  transfers between devices with their start and end apart: 3, of which 3 were waited for; matrix products, arithmetic and copies ran while one was open for 5% of the time, Pallas kernels for 2%

profile of v1, /device:TPU:0, one launch (start us, length us, event | category | flops | bytes accessed | tf_op | source)
XLA Modules:
  0.0 489.0 jit_solution(18058332673370047703)
XLA Ops:
  8.0 0.0 all-gather.3.cloned.1.call-start
  8.0 1.7 pad_maximum_fusion
  9.7 0.0 all-gather.3.cloned.1.call-update
  9.7 0.0 all-reduce.3.cloned.1.call-start
  9.8 58.8 %all-gather.3.cloned.1.call-done = bf16[3584,512]{1,0:T(8,128)(2,1)} async-done(((bf16[224,512]{1,0:T(8,128)(2,1)}), bf16[3584,512]{1,0:T(8,128)(2,1)}) %all-gather.3.cloned.1.call-update) | async-done | bytes 3670032 | tf_op jit(solution)/shard_map/all_gather | solution.py:55
  68.5 0.0 copy-start.1
  68.6 6.4 %fusion = f32[512,512]{1,0:T(8,128)} fusion(bf16[3584,512]{1,0:T(8,128)(2,1)} %all-gather.3.cloned.1.call-done), kind=kOutput, calls=%fused_computation.5 | convolution fusion | flops 1879048192 | bytes 4718592 | tf_op jit(solution)/shard_map/dot_general | solution.py:12
  74.9 0.0 copy-done.1
  74.9 11.8 %convolution_bitcast_fusion = f32[1792,512]{0,1:T(8,128)} fusion(bf16[3584,512]{1,0:T(8,128)(2,1)S(1)} %copy-done.1, bf16[1792,3584]{1,0:T(8,128)(2,1)} %param.4), kind=kOutput, calls=%fused_computation.1 | convolution fusion | flops 6576668672 | bytes 20185088 | tf_op jit(solution)/shard_map/dot_general | solution.py:57
  86.7 0.0 all-reduce.3.cloned.1.call-update
  86.7 0.2 all-gather.5.cloned.1.call-start
  87.0 0.3 all-gather.5.cloned.1.call-update
  87.3 126.4 %all-reduce.3.cloned.1.call-done = (f32[1792,512]{0,1:T(8,128)}, f32[512,512]{1,0:T(8,128)}) async-done(((f32[1792,512]{0,1:T(8,128)}, f32[512,512]{1,0:T(8,128)}), (f32[1792,512]{0,1:T(8,128)}, f32[512,512]{1,0:T(8,128)})) %all-reduce.3.cloned.1.call-update) | async-done | bytes 4718608 | tf_op jit(solution)/shard_map/psum | solution.py:58
  213.7 0.0 copy-start
  213.7 1.2 copy-done
  214.9 10.7 %block_inverse.1 = f32[512,512]{1,0:T(8,128)S(1)} custom-call(f32[512,512]{1,0:T(8,128)S(1)} %copy-done), custom_call_target="tpu_custom_call" | custom-call | tf_op jit(solution)/shard_map/block_inverse/pallas_call | solution.py:43
  225.6 0.0 copy-start.2
  225.6 8.0 %convolution_convert_fusion = bf16[1792,512]{1,0:T(8,128)(2,1)S(1)} fusion(f32[1792,512]{0,1:T(8,128)} %get-tuple-element.2, f32[512,512]{1,0:T(8,128)S(1)} %block_inverse.1), kind=kOutput, calls=%fused_computation.2 | convolution fusion | flops 5638062080 | bytes 6553600 | tf_op jit(solution)/shard_map/dot_general | solution.py:18
  233.7 0.0 copy-done.2
  233.7 12.7 %subtract_convert_fusion = bf16[1792,3584]{1,0:T(8,128)(2,1)} fusion(bf16[1792,3584]{1,0:T(8,128)(2,1)} %param.4, bf16[1792,512]{1,0:T(8,128)(2,1)S(1)} %convolution_convert_fusion, bf16[3584,512]{1,0:T(8,128)(2,1)S(1)} %copy-done.2), kind=kOutput, calls=%fused_computation | convolution fusion | flops 6595936256 | bytes 31195136 | tf_op jit(solution)/shard_map/dot_general | solution.py:60
  246.4 180.8 %all_to_all.19 = bf16[8,224,3584]{2,1,0:T(8,128)(2,1)S(1)} all-to-all(bf16[8,224,3584]{2,1,0:T(8,128)(2,1)} %bitcast.19), channel_id=1, replica_groups=mesh['row'=8,'col'=16] {'row'}, dimensions={0} | all-to-all | bytes 25690112 | tf_op jit(solution)/shard_map/all_to_all | solution.py:64
  427.2 5.5 %copy.7 = bf16[8,28,8,3584]{3,2,0,1:T(8,128)(2,1)} copy(bf16[8,28,8,3584]{3,2,1,0:T(8,128)(2,1)S(1)} %bitcast.16) | data formatting | bytes 25690112 | tf_op jit(solution)/shard_map/all_to_all | solution.py:64
  432.7 35.9 %all-gather.5.cloned.1.call-done = bf16[256,28672]{0,1:T(8,128)(2,1)} async-done(((bf16[256,224]{0,1:T(8,128)(2,1)}), bf16[256,28672]{0,1:T(8,128)(2,1)}) %all-gather.5.cloned.1.call-update) | async-done | bytes 14680080 | tf_op jit(solution)/shard_map/all_gather | solution.py:67
  468.6 12.9 %convolution_convert_fusion.1 = bf16[224,256]{1,0:T(8,128)(2,1)} fusion(bf16[224,28672]{1,0:T(8,128)(2,1)} %bitcast.17, bf16[256,28672]{0,1:T(8,128)(2,1)} %all-gather.5.cloned.1.call-done), kind=kOutput, calls=%fused_computation.3 | convolution fusion | flops 3288391680 | bytes 27639808 | tf_op jit(solution)/shard_map/dot_general | solution.py:65
Async XLA Ops:
  8.0 60.6 %all-gather.3.cloned.1.call-start = ((), (), s32[]{:S(2)}) async-start(), calls=%async_computation.1 | async-start | bytes 3899392 | tf_op jit(solution)/shard_map/all_gather | solution.py:55
  9.7 204.0 %all-reduce.3.cloned.1.call-start = ((), (), s32[]{:S(2)}) async-start(), calls=%async_computation.3 | async-start | bytes 9437184 | tf_op jit(solution)/shard_map/psum | solution.py:58
  68.5 6.4 %copy-start.1 = (bf16[3584,512]{1,0:T(8,128)(2,1)S(1)}, bf16[3584,512]{1,0:T(8,128)(2,1)}, u32[]{:S(2)}) copy-start(bf16[3584,512]{1,0:T(8,128)(2,1)} %all-gather.3.cloned.1.call-done) | copy-start | bytes 11010052
  86.7 381.9 %all-gather.5.cloned.1.call-start = ((), (), s32[]{:S(2)}) async-start(), calls=%async_computation.2 | async-start | bytes 14794752 | tf_op jit(solution)/shard_map/all_gather | solution.py:67
  213.7 1.2 copy-start
  225.6 8.0 %copy-start.2 = (bf16[3584,512]{1,0:T(8,128)(2,1)S(1)}, bf16[3584,512]{1,0:T(8,128)(2,1)}, u32[]{:S(2)}) copy-start(bf16[3584,512]{1,0:T(8,128)(2,1)} %all-gather.3.cloned.1.call-done) | copy-start | bytes 11010052
Sparse Core Ops, SparseCore 0:
  11.8 56.6 all-gather.2
  86.9 126.7 all-reduce.2
Sparse Core Ops, SparseCore 1:
  88.9 379.6 all-gather.4

commit v2 on v1

--- a/solution.py
+++ b/solution.py
@@ -4,6 +4,207 @@
 from jax.experimental import pallas as pl
 from jax.experimental.pallas import tpu as pltpu
 from jax.sharding import PartitionSpec as P
+
+MESH = pl.DeviceIdType.MESH
+PARTS = 7
+SLOTS = 144
+
+
+def place():
+    row, col = lax.axis_index("row"), lax.axis_index("col")
+    return row // 4, row % 4, col // 4, (col // 2) % 2, col % 2
+
+
+def device(zl, x, y, zh, k):
+    return (zl * 4 + lax.rem(x + 4, 4), lax.rem(y + 4, 4) * 4 + zh * 2 + k)
+
+
+class Transfers:
+    def __init__(self, send_sem, recv_sem):
+        self.send_sem, self.recv_sem = send_sem, recv_sem
+        self.count = 0
+        self.pending_send, self.pending_recv = {}, {}
+
+    def start(self, source, target, to, arrival=None):
+        slot = self.count
+        self.count += 1
+        copy = pltpu.make_async_remote_copy(
+            source, target, self.send_sem.at[slot], self.recv_sem.at[slot],
+            device_id=to, device_id_type=MESH,
+        )
+        copy.start()
+        self.pending_send[slot] = copy
+        self.pending_recv[slot] = copy
+        return slot
+
+    def received(self, slot):
+        if slot in self.pending_recv:
+            self.pending_recv.pop(slot).wait_recv()
+
+    def sent(self, slot):
+        if slot in self.pending_send:
+            self.pending_send.pop(slot).wait_send()
+
+    def finish(self):
+        for slot in list(self.pending_recv):
+            self.received(slot)
+        for slot in list(self.pending_send):
+            self.sent(slot)
+
+
+def comm_kernel(e_ref, s_ref, g_ref, x_ref, sf_ref, gf_ref, send_sem, recv_sem, local_sem):
+    zl, x, y, zh, k = place()
+    me = zl * 4 + x
+    sib = device(zl, x, y, zh, 1 - k)
+    cross = device(1 - zl, x, y, 1 - zh, k)
+    partners = [device(a, x + d, y, zh, k) for a, d in
+                [(1 - zl, 0), (zl, 1), (zl, 3), (1 - zl, 1), (1 - zl, 3), (zl, 2), (1 - zl, 2)]]
+    barrier = pltpu.get_barrier_semaphore()
+    everyone = partners + [sib, cross] + [device(zl, x, y + d, zh, k) for d in (1, 2, 3)]
+    for to in everyone:
+        pl.semaphore_signal(barrier, inc=1, device_id=to, device_id_type=MESH)
+    pl.semaphore_wait(barrier, len(everyone))
+
+    t = Transfers(send_sem, recv_sem)
+    rows, width = x_ref.shape[0], e_ref.shape[1]
+
+    own_columns = pl.ds(pl.multiple_of(me * width, 128), width)
+    mine = pltpu.make_async_copy(
+        e_ref.at[pl.ds(pl.multiple_of(me * rows, 16), rows)], x_ref.at[:, own_columns], local_sem.at[0])
+    mine_s = pltpu.make_async_copy(s_ref, sf_ref.at[zl, x, y, zh, k], local_sem.at[1])
+    mine_g = pltpu.make_async_copy(g_ref, gf_ref.at[zl, x, y, zh, k], local_sem.at[2])
+
+    piece = rows // PARTS
+    batches = []
+
+    def batch():
+        q = len(batches)
+        slots = []
+        if q < PARTS:
+            for to in partners:
+                theirs = to[0]
+                src = e_ref.at[pl.ds(pl.multiple_of(theirs * rows + q * piece, 16), piece)]
+                dst = x_ref.at[pl.ds(q * piece, piece), own_columns]
+                slots.append(t.start(src, dst, to))
+        batches.append(slots)
+
+    def push(ref, index, to):
+        view = ref.at[index]
+        return t.start(view, view, to)
+
+    def share(ref, index):
+        return push(ref, index, sib)
+
+    full = slice(None)
+    mine_s.start()
+    mine_g.start()
+    mine.start()
+    own = (zl, x, y, zh, k)
+    a1 = t.start(s_ref, sf_ref.at[own], device(1 - zl, x, y, zh, k))
+    a2a = [t.start(s_ref, sf_ref.at[own], device(zl, x + d, y, zh, k)) for d in (1, 3, 2)]
+    b1 = [t.start(g_ref, gf_ref.at[own], device(zl, x + d, y, zh, k)) for d in (1, 3, 2)]
+    t.start(s_ref, sf_ref.at[own], sib)
+    t.start(g_ref, gf_ref.at[own], sib)
+    batch()
+    mine_s.wait()
+    mine_g.wait()
+    t.received(a1)
+    other = (1 - zl, x, y, zh, k)
+    a2b = [push(sf_ref, other, device(zl, x + d, y, zh, k)) for d in (1, 3, 2)]
+    for s in a2a:
+        t.received(s)
+    a3a = push(sf_ref, (zl, full, y, zh, k), cross)
+    a4a = [[push(sf_ref, (zl, full, y, zh, k), device(zl, x, y + d, zh, k)) for d in (1, 3)]]
+    for s in b1:
+        t.received(s)
+    b2 = push(gf_ref, (zl, full, y, zh, k), device(1 - zl, x, y, zh, k))
+    for s in a2b:
+        t.received(s)
+    a3b = push(sf_ref, (1 - zl, full, y, zh, k), cross)
+    a4a.append([push(sf_ref, (1 - zl, full, y, zh, k), device(zl, x, y + d, zh, k)) for d in (1, 3)])
+    t.received(b2)
+    b3 = {d: push(gf_ref, (full, full, y, zh, k), device(zl, x, y + d, zh, k)) for d in (1, 3, 2)}
+    b4 = [push(gf_ref, (full, full, y, zh, k), cross)]
+    for d in (1, 2, 3):
+        share(sf_ref, (full, lax.rem(x + d, 4), y, zh, k))
+        share(gf_ref, (full, lax.rem(x + d, 4), y, zh, k))
+    share(sf_ref, other)
+    share(gf_ref, other)
+    batch()
+    t.received(a3a)
+    a4b = [[push(sf_ref, (1 - zl, full, y, 1 - zh, k), device(zl, x, y + d, zh, k)) for d in (1, 3)]]
+    t.received(a3b)
+    a4b.append([push(sf_ref, (zl, full, y, 1 - zh, k), device(zl, x, y + d, zh, k)) for d in (1, 3)])
+    share(sf_ref, (full, full, y, 1 - zh, k))
+    batch()
+    up, down, far = lax.rem(y + 1, 4), lax.rem(y + 3, 4), lax.rem(y + 2, 4)
+    source_of = {1: down, 3: up, 2: far}
+    far_own, far_other = [], []
+    for part, a in ((0, zl), (1, 1 - zl)):
+        t.received(a4a[part][0])
+        far_own.append(push(sf_ref, (a, full, down, zh, k), device(zl, x, y + 1, zh, k)))
+    for d in (1, 3):
+        t.received(b3[d])
+        b4.append(push(gf_ref, (full, full, source_of[d], zh, k), cross))
+        share(gf_ref, (full, full, source_of[d], zh, k))
+    for part in (0, 1):
+        t.received(a4a[part][1])
+    share(sf_ref, (full, full, down, zh, k))
+    share(sf_ref, (full, full, up, zh, k))
+    batch()
+    t.received(b3[2])
+    b4.append(push(gf_ref, (full, full, far, zh, k), cross))
+    share(gf_ref, (full, full, far, zh, k))
+    batch()
+    for part, a in ((0, 1 - zl), (1, zl)):
+        t.received(a4b[part][1])
+        far_other.append(push(sf_ref, (a, full, up, 1 - zh, k), device(zl, x, y + 3, zh, k)))
+    t.received(b4[0])
+    share(gf_ref, (full, full, y, 1 - zh, k))
+    for part in (0, 1):
+        t.received(a4b[part][0])
+    share(sf_ref, (full, full, down, 1 - zh, k))
+    share(sf_ref, (full, full, up, 1 - zh, k))
+    batch()
+    batch()
+    for i, d in ((1, 1), (2, 3)):
+        t.received(b4[i])
+        share(gf_ref, (full, full, source_of[d], 1 - zh, k))
+    for slot in far_own:
+        t.received(slot)
+    share(sf_ref, (full, full, far, zh, k))
+    t.received(b4[3])
+    share(gf_ref, (full, full, far, 1 - zh, k))
+    for slot in far_other:
+        t.received(slot)
+    share(sf_ref, (full, full, far, 1 - zh, k))
+    t.finish()
+    mine.wait()
+
+
+def exchange(eigenvectors, sets, gradient):
+    blocks = (2, 4, 4, 2, 2)
+    rows, width = eigenvectors.shape[0] // 8, eigenvectors.shape[1]
+    return pl.pallas_call(
+        comm_kernel,
+        out_shape=(
+            jax.ShapeDtypeStruct((rows, 8 * width), jnp.bfloat16),
+            jax.ShapeDtypeStruct(blocks + sets.shape, jnp.bfloat16),
+            jax.ShapeDtypeStruct(blocks + gradient.shape, jnp.bfloat16),
+        ),
+        in_specs=[pl.BlockSpec(memory_space=pl.ANY)] * 3,
+        out_specs=(pl.BlockSpec(memory_space=pl.ANY),) * 3,
+        scratch_shapes=[
+            pltpu.SemaphoreType.DMA((SLOTS,)),
+            pltpu.SemaphoreType.DMA((SLOTS,)),
+            pltpu.SemaphoreType.DMA((3,)),
+        ],
+        compiler_params=pltpu.CompilerParams(
+            collective_id=0, has_side_effects=True, vmem_limit_bytes=48 * 1024 * 1024
+        ),
+        name="exchange",
+    )(eigenvectors, sets, gradient)
+
 
 HIGH = lax.Precision.HIGHEST
 
@@ -52,23 +253,18 @@
 
 def body(eigenvectors, reflectors_first, reflectors_second, forget_gradient):
     own_sets = jnp.concatenate([reflectors_first, reflectors_second], axis=1)
-    both_sets = lax.all_gather(own_sets, "col", axis=0, tiled=True)
-    gram = lax.psum(inner_products(both_sets, both_sets), "row")
-    products = jnp.dot(eigenvectors, both_sets, preferred_element_type=jnp.float32)
-    products = lax.psum(products, "row")
+    slab, all_sets, all_gradient = exchange(eigenvectors, own_sets, forget_gradient.T)
+    all_sets = all_sets.reshape(-1, own_sets.shape[1])
+    all_gradient = all_gradient.reshape(-1, forget_gradient.shape[0])
+    gram = inner_products(all_sets, all_sets)
+    products = jnp.dot(slab, all_sets, preferred_element_type=jnp.float32)
     coefficients = exact(products, block_inverse(gram)).astype(jnp.bfloat16)
     update = lax.dot_general(
-        coefficients, both_sets, (((1,), (1,)), ((), ())), preferred_element_type=jnp.float32
+        coefficients, all_sets, (((1,), (1,)), ((), ())), preferred_element_type=jnp.float32
     )
-    renewed = (eigenvectors.astype(jnp.float32) - update).astype(jnp.bfloat16)
-    eig_slab = lax.all_to_all(renewed, "row", split_axis=0, concat_axis=1, tiled=True)
-    rotated = lax.dot_general(
-        eig_slab,
-        lax.all_gather(forget_gradient, ("row", "col"), axis=1, tiled=True),
-        (((1,), (1,)), ((), ())),
-        preferred_element_type=jnp.float32,
-    )
-    return (eig_slab, rotated.astype(jnp.bfloat16))
+    renewed = (slab.astype(jnp.float32) - update).astype(jnp.bfloat16)
+    rotated = jnp.dot(renewed, all_gradient, preferred_element_type=jnp.float32)
+    return (renewed, rotated.astype(jnp.bfloat16))
 
 
 def solution(mesh):

time: 490 us -> 299 us (0.61)
  waiting for transfers between devices: 221 us -> 0 us
  Pallas kernels: 10.7 us -> 216 us
  blocking collectives: 181 us -> 0 us
  matrix products: 51.9 us -> 78.2 us
  between operations: 15.5 us -> 0.68 us
  local copies, waits for them, and re-layouts: 6.75 us -> 0.89 us
    pallas_call x0 -> x1, Pallas kernels: none -> 206 us  [exchange(): pl.pallas_call(comm_kernel, out_shape=(jax.ShapeDtypeStruct((rows, 8 * wi...]
    all_to_all x1 -> x0, blocking collectives: 181 us -> none  [body(): lax.all_to_all(renewed, 'row', split_axis=0, concat_axis=1, tiled=True)]
    psum x1 -> x0, waiting for transfers between devices: 126 us -> none  [body(): products = lax.psum(products, 'row')]
    all_gather x2 -> x0, waiting for transfers between devices: 94.7 us -> none  [the longest x1 58.8 us: body(): both_sets = lax.all_gather(own_sets, 'col', axis=0, tiled=True)]
    dot_general x1, matrix products: 6.36 us -> 27.8 us  [inner_products(): lax.dot_general(left_side, right_side, (((0,), (0,)), ((), ())), preferre...]
    dot_general x3, matrix products: 37.5 us -> 49.4 us  [the longest x1 19.9 us: body(): lax.dot_general(coefficients, all_sets, (((1,), (1,)), ((), ())), preferr...]
    dot_general x1, matrix products: 8.03 us -> 0.96 us  [exact(): jnp.dot(left_side, right_side, precision=HIGH, preferred_element_type=jnp...]
    all_to_all x1 -> x0, local copies, waits for them, and re-layouts: 5.5 us -> none  [body(): lax.all_to_all(renewed, 'row', split_axis=0, concat_axis=1, tiled=True)]
  transfers between devices with their start and end apart: 3 -> 0, of which waited for: 3 -> 0; matrix products, arithmetic and copies ran while one was open for 5% -> 0% of each run, Pallas kernels for 2% -> 0%
where the time goes in v2:
time: 299 us; the launch traced here: 297 us
  Pallas kernels  216 us (72%)
  matrix products  78.2 us (26%)
    pallas_call x1, Pallas kernels, exchange(): pl.pallas_call(comm_kernel, out_shape=(jax.ShapeDtypeStruct((rows, 8 * wi...  206 us
    dot_general x1, matrix products, inner_products(): lax.dot_general(left_side, right_side, (((0,), (0,)), ((), ())), preferre...  27.8 us
    dot_general x1, matrix products, body(): lax.dot_general(coefficients, all_sets, (((1,), (1,)), ((), ())), preferr...  19.9 us
    dot_general x1, matrix products, body(): products = jnp.dot(slab, all_sets, preferred_element_type=jnp.float32)  16.6 us
    dot_general x1, matrix products, body(): rotated = jnp.dot(renewed, all_gradient, preferred_element_type=jnp.float32)  12.9 us
    pallas_call x1, Pallas kernels, block_inverse(): pl.pallas_call(inverse_kernel, out_shape=jax.ShapeDtypeStruct(gram.shape,...  10.7 us

profile of v2, /device:TPU:0, one launch (start us, length us, event | category | flops | bytes accessed | tf_op | source)
XLA Modules:
  0.0 297.1 jit_solution(4792999633834350860)
XLA Ops:
  0.6 1.0 pad_maximum_fusion.s_ref
  1.6 0.0 copy-start
  1.6 0.9 copy-done
  2.5 205.7 %exchange.1 = (bf16[224,28672]{1,0:T(8,128)(2,1)}, bf16[2,4,4,2,2,224,512]{6,5,4,3,2,1,0:T(8,128)(2,1)}, bf16[2,4,4,2,2,224,256]{6,5,4,3,2,1,0:T(8,128)(2,1)}) custom-call(bf16[1792,3584]{1,0:T(8,128)(2,1)} %e_ref.1, bf16[224,512]{1,0:T(8,128)(2,1)S(1)} %pad_maximum_fusion.s_ref, bf16[224,256]{1,0:T(8,128)(2,1)S(1)} %bitcast.17), custom_call_target="tpu_custom_call" | custom-call | tf_op jit(solution)/shard_map/exchange/pallas_call | solution.py:188
  208.3 16.6 %fusion.1 = f32[224,512]{1,0:T(8,128)S(1)} fusion(bf16[224,28672]{1,0:T(8,128)(2,1)} %get-tuple-element.5, bf16[28672,512]{1,0:T(8,128)(2,1)} %bitcast.18), kind=kOutput, calls=%fused_computation.6 | convolution fusion | flops 6576668672 | bytes 42663936 | tf_op jit(solution)/shard_map/dot_general | solution.py:260
  224.8 27.8 %convolution_bitcast_fusion.gram_ref = f32[512,512]{1,0:T(8,128)S(1)} fusion(bf16[2,4,4,2,2,224,512]{6,5,4,3,2,1,0:T(8,128)(2,1)} %get-tuple-element.6), kind=kOutput, calls=%fused_computation.2 | convolution fusion | flops 15032385536 | bytes 30408704 | tf_op jit(solution)/shard_map/dot_general | solution.py:213
  252.6 10.7 %block_inverse.1 = f32[512,512]{1,0:T(8,128)S(1)} custom-call(f32[512,512]{1,0:T(8,128)S(1)} %convolution_bitcast_fusion.gram_ref), custom_call_target="tpu_custom_call" | custom-call | tf_op jit(solution)/shard_map/block_inverse/pallas_call | solution.py:244
  263.3 1.0 convolution_convert_fusion
  264.3 19.9 %fusion = bf16[224,28672]{1,0:T(8,128)(2,1)} fusion(bf16[224,512]{1,0:T(8,128)(2,1)S(1)} %convolution_convert_fusion, bf16[28672,512]{1,0:T(8,128)(2,1)} %bitcast.19, bf16[224,28672]{1,0:T(8,128)(2,1)} %get-tuple-element.5), kind=kOutput, calls=%fused_computation.1 | convolution fusion | flops 6595936256 | bytes 55279616 | tf_op jit(solution)/shard_map/dot_general | solution.py:262
  284.2 12.9 %convolution_convert_fusion.1 = bf16[224,256]{1,0:T(8,128)(2,1)} fusion(bf16[224,28672]{1,0:T(8,128)(2,1)} %fusion, bf16[28672,256]{1,0:T(8,128)(2,1)} %bitcast.20), kind=kOutput, calls=%fused_computation.4 | convolution fusion | flops 3288391680 | bytes 27639808 | tf_op jit(solution)/shard_map/dot_general | solution.py:266
Async XLA Ops:
  1.6 0.9 copy-start

commit v3 on v1

v3 whole, which is shorter than its diff:
```python
import jax
import jax.numpy as jnp
from jax import lax
from jax.experimental import pallas as pl
from jax.experimental.pallas import tpu as pltpu
from jax.sharding import PartitionSpec as P

MESH = pl.DeviceIdType.MESH
HIGH = lax.Precision.HIGHEST
BATCHES = 7
SLOTS = 160
SPLIT = 384
UPPER = 128


def exact(left_side, right_side):
    return jnp.dot(left_side, right_side, precision=HIGH, preferred_element_type=jnp.float32)


def inner_products(left_side, right_side):
    return lax.dot_general(
        left_side, right_side, (((0,), (0,)), ((), ())), preferred_element_type=jnp.float32
    )


def invert_upper(gram, inverse_ref):
    half = gram.shape[0] // 2
    rows = lax.broadcasted_iota(jnp.int32, (half, half), 0)
    cols = lax.broadcasted_iota(jnp.int32, (half, half), 1)
    parts = [gram[:half, :half], gram[half:, half:]]
    inverses = [jnp.where(rows == cols, 2.0 / part, 0.0) for part in parts]
    for level in range(half.bit_length() - 1):
        row_block, col_block = lax.shift_right_logical(rows, level), lax.shift_right_logical(cols, level)
        corner = (row_block + 1 == col_block) & ((row_block & 1) == 0)
        corners = [jnp.where(corner, part, 0.0) for part in parts]
        steps = [exact(c, i) for c, i in zip(corners, inverses)]
        inverses = [i - exact(i, s) for i, s in zip(inverses, steps)]
    cross = exact(inverses[0], exact(gram[:half, half:], inverses[1]))
    inverse_ref[:half, :half] = inverses[0]
    inverse_ref[half:, half:] = inverses[1]
    inverse_ref[:half, half:] = -cross
    inverse_ref[half:, :half] = jnp.zeros((half, half), jnp.float32)


def place():
    row, col = lax.axis_index("row"), lax.axis_index("col")
    return row // 4, row % 4, col // 4, (col // 2) % 2, col % 2


def device(zl, x, y, zh, k):
    return (zl * 4 + lax.rem(x + 4, 4), lax.rem(y + 4, 4) * 4 + zh * 2 + k)


class Transfers:
    def __init__(self, send_sem, recv_sem):
        self.send_sem, self.recv_sem = send_sem, recv_sem
        self.count = 0
        self.pending_send, self.pending_recv = {}, {}

    def start(self, source, target, to):
        slot = self.count
        self.count += 1
        copy = pltpu.make_async_remote_copy(
            source, target, self.send_sem.at[slot], self.recv_sem.at[slot],
            device_id=to, device_id_type=MESH,
        )
        copy.start()
        self.pending_send[slot] = copy
        self.pending_recv[slot] = copy
        return slot

    def received(self, *slots):
        for slot in slots:
            if slot in self.pending_recv:
                self.pending_recv.pop(slot).wait_recv()

    def finish(self):
        self.received(*list(self.pending_recv))
        for copy in self.pending_send.values():
            copy.wait_send()


def exchange_kernel(
    e_ref, s_ref, g_ref, x_ref, sf_ref, gf_ref, coef_ref, rot_ref,
    send_sem, recv_sem, local_sem, part, from_y, y_sum, from_z, sums, inverse, total,
):
    zl, x, y, zh, k = place()
    me = zl * 4 + x
    sib = device(zl, x, y, zh, 1 - k)
    cross = device(1 - zl, x, y, 1 - zh, k)
    flip = device(zl, x, y, 1 - zh, k)
    other_z = device(1 - zl, x, y, zh, k)
    near_x = [device(zl, x + d, y, zh, k) for d in (1, 3, 2)]
    near_y = {d: device(zl, x, y + d, zh, k) for d in (1, 3, 2)}
    partners = [device(a, x + d, y, zh, k) for a, d in
                [(1 - zl, 0), (zl, 1), (zl, 3), (1 - zl, 1), (1 - zl, 3), (zl, 2), (1 - zl, 2)]]
    barrier = pltpu.get_barrier_semaphore()
    everyone = partners + [sib, cross, flip] + list(near_y.values())
    for to in everyone:
        pl.semaphore_signal(barrier, inc=1, device_id=to, device_id_type=MESH)
    pl.semaphore_wait(barrier, len(everyone))

    t = Transfers(send_sem, recv_sem)
    rows, width = x_ref.shape[0], e_ref.shape[1]
    own_columns = pl.ds(pl.multiple_of(me * width, 128), width)
    piece = rows // BATCHES
    batches = []
    full = slice(None)

    def batch():
        q = len(batches)
        slots = []
        for to in partners:
            source = e_ref.at[pl.ds(pl.multiple_of(to[0] * rows + q * piece, 16), piece)]
            slots.append(t.start(source, x_ref.at[pl.ds(q * piece, piece), own_columns], to))
        batches.append(slots)

    def push(ref, index, to):
        view = ref.at[index]
        return t.start(view, view, to)

    def share(ref, index):
        return push(ref, index, sib)

    mine = pltpu.make_async_copy(
        e_ref.at[pl.ds(pl.multiple_of(me * rows, 16), rows)], x_ref.at[:, own_columns], local_sem.at[0])
    mine_s = pltpu.make_async_copy(s_ref, sf_ref.at[zl, x, y, zh, k], local_sem.at[1])
    mine_g = pltpu.make_async_copy(g_ref, gf_ref.at[zl, x, y, zh, k], local_sem.at[2])

    def group_sums():
        part[...] = jnp.zeros_like(part)

        def step(s_block, g_block):
            s_value = s_block[...].reshape(-1, SPLIT)
            g_value = g_block[...].reshape(-1, g_block.shape[-1])
            sets = jnp.concatenate([s_value, g_value[:, :UPPER]], axis=1)
            part[:, :SPLIT] += inner_products(sets, s_value)
            part[:, SPLIT:] += inner_products(sets, g_value)

        def spec(ref):
            return pl.BlockSpec(
                (None, None, None, None, 2) + ref.shape[5:], lambda i: (i // 4, i % 4, y, zh, 0, 0, 0)
            )

        pltpu.emit_pipeline(step, grid=(8,), in_specs=[spec(sf_ref), spec(gf_ref)])(sf_ref, gf_ref)

    def add_products(y_block, low, high):
        def step(x_block, s_block, g_block):
            x_value = x_block[...]
            s_value = s_block[...].reshape(-1, SPLIT)
            g_value = g_block[...].reshape(-1, g_block.shape[-1])
            total[low:high, :SPLIT] += jnp.dot(x_value, s_value, preferred_element_type=jnp.float32)
            total[low:high, SPLIT:] += jnp.dot(x_value, g_value, preferred_element_type=jnp.float32)

        def spec(ref):
            return pl.BlockSpec(
                (None, None, None, 2, 2) + ref.shape[5:], lambda i: (i // 4, i % 4, y_block, 0, 0, 0, 0)
            )

        x_rows = x_ref.at[pl.ds(low, high - low)]
        x_spec = pl.BlockSpec((high - low, width // 4), lambda i: (0, i * 4 + y_block))
        pltpu.emit_pipeline(step, grid=(8,), in_specs=[x_spec, spec(sf_ref), spec(gf_ref)])(
            x_rows, sf_ref, gf_ref)

    mine_s.start()
    mine_g.start()
    own, other = (zl, x, y, zh, k), (1 - zl, x, y, zh, k)
    a1 = t.start(s_ref, sf_ref.at[own], other_z)
    a2a = [t.start(s_ref, sf_ref.at[own], to) for to in near_x]
    b1 = [t.start(g_ref, gf_ref.at[own], to) for to in near_x]
    home = [t.start(s_ref, sf_ref.at[own], sib), t.start(g_ref, gf_ref.at[own], sib)]
    batch()
    mine.start()
    total[...] = jnp.zeros_like(total)
    mine_s.wait()
    mine_g.wait()
    t.received(a1)
    a2b = [push(sf_ref, other, to) for to in near_x]
    t.received(*a2a)
    a3 = [push(sf_ref, (zl, full, y, zh, k), cross)]
    a4a = [[push(sf_ref, (zl, full, y, zh, k), near_y[d]) for d in (1, 3)]]
    t.received(*b1)
    b2 = push(gf_ref, (zl, full, y, zh, k), other_z)
    t.received(*a2b)
    a3.append(push(sf_ref, (1 - zl, full, y, zh, k), cross))
    a4a.append([push(sf_ref, (1 - zl, full, y, zh, k), near_y[d]) for d in (1, 3)])
    t.received(b2)
    b3 = {d: push(gf_ref, (full, full, y, zh, k), near_y[d]) for d in (1, 3, 2)}
    b4 = {0: push(gf_ref, (full, full, y, zh, k), cross)}
    home += [share(ref, other) for ref in (sf_ref, gf_ref)]
    home += [share(ref, (full, lax.rem(x + d, 4), y, zh, k)) for d in (1, 2, 3) for ref in (sf_ref, gf_ref)]
    batch()
    t.received(*home)
    group_sums()
    slice_rows = pl.ds(pl.multiple_of((me * 2 + k) * 32, 32), 32)
    y_parts = [t.start(part.at[slice_rows], from_y.at[d - 1], near_y[d]) for d in (1, 2, 3)]

    t.received(a3[0])
    a4b = [[push(sf_ref, (1 - zl, full, y, 1 - zh, k), near_y[d]) for d in (1, 3)]]
    t.received(a3[1])
    a4b.append([push(sf_ref, (zl, full, y, 1 - zh, k), near_y[d]) for d in (1, 3)])
    ready = {0: [share(sf_ref, (full, full, y, 1 - zh, k))]}
    batch()
    t.received(*y_parts)
    y_sum[...] = part[slice_rows, :] + from_y[0] + from_y[1] + from_y[2]
    z_part = t.start(y_sum, from_z, flip)

    source = {1: lax.rem(y + 3, 4), 3: lax.rem(y + 1, 4), 2: lax.rem(y + 2, 4)}
    far_own, far_other = [], []
    for half, a in ((0, zl), (1, 1 - zl)):
        t.received(a4a[half][0])
        far_own.append(push(sf_ref, (a, full, source[1], zh, k), near_y[1]))
    t.received(z_part)
    sums[zl, x, k] = y_sum[...] + from_z[...]
    x_sums = [push(sums, (zl, x, k), to) for to in near_x]
    for d in (1, 3):
        t.received(b3[d])
        b4[d] = push(gf_ref, (full, full, source[d], zh, k), cross)
        ready[d] = [b4[d], share(gf_ref, (full, full, source[d], zh, k))]
    t.received(a4a[0][1], a4a[1][1])
    for d in (1, 3):
        ready[d].append(share(sf_ref, (full, full, source[d], zh, k)))
    batch()
    t.received(*x_sums)
    z_sums = push(sums, (zl, full, k), other_z)
    t.received(b3[2])
    b4[2] = push(gf_ref, (full, full, source[2], zh, k), cross)
    ready[2] = [b4[2], share(gf_ref, (full, full, source[2], zh, k))]
    batch()
    t.received(z_sums)
    sib_sums = push(sums, (full, full, k), sib)
    t.received(b4[0])
    ready[0].append(share(gf_ref, (full, full, y, 1 - zh, k)))
    batch()
    t.received(sib_sums)
    invert_upper(sums[...].reshape(512, 768)[:, :512], inverse)
    for half, a in ((0, 1 - zl), (1, zl)):
        t.received(a4b[half][1])
        far_other.append(push(sf_ref, (a, full, source[3], 1 - zh, k), near_y[3]))
    t.received(a4b[0][0], a4b[1][0])
    for d in (1, 3):
        ready[d].append(share(sf_ref, (full, full, source[d], 1 - zh, k)))
    batch()
    mine.wait()
    for slots in batches[:4]:
        t.received(*slots)
    t.received(*ready[0])
    add_products(y, 0, 4 * piece)
    t.received(*far_own)
    ready[2].append(share(sf_ref, (full, full, source[2], zh, k)))
    for d in (1, 3):
        t.received(b4[d])
        ready[d].append(share(gf_ref, (full, full, source[d], 1 - zh, k)))
    for d in (1, 3):
        t.received(*ready[d])
        add_products(source[d], 0, 4 * piece)
    t.received(b4[2])
    ready[2].append(share(gf_ref, (full, full, source[2], 1 - zh, k)))
    t.received(*far_other)
    ready[2].append(share(sf_ref, (full, full, source[2], 1 - zh, k)))
    for slots in batches[4:]:
        t.received(*slots)
    for block in (y, source[1], source[3]):
        add_products(block, 4 * piece, rows)
    t.finish()
    add_products(source[2], 0, rows)
    coefficients = exact(total[:, :512], inverse[...]).astype(jnp.bfloat16)
    coef_ref[...] = coefficients
    changed = exact(coefficients.astype(jnp.float32), sums[...].reshape(512, 768)[:, 512:])
    rot_ref[...] = (total[:, 512:] - changed).astype(jnp.bfloat16)


def exchange(eigenvectors, sets, gradient):
    blocks = (2, 4, 4, 2, 2)
    rows, width = eigenvectors.shape[0] // 8, eigenvectors.shape[1]
    any_space = pl.BlockSpec(memory_space=pl.ANY)
    vmem = pl.BlockSpec(memory_space=pltpu.VMEM)
    return pl.pallas_call(
        exchange_kernel,
        out_shape=(
            jax.ShapeDtypeStruct((rows, 8 * width), jnp.bfloat16),
            jax.ShapeDtypeStruct(blocks + sets.shape, jnp.bfloat16),
            jax.ShapeDtypeStruct(blocks + gradient.shape, jnp.bfloat16),
            jax.ShapeDtypeStruct((rows, 512), jnp.bfloat16),
            jax.ShapeDtypeStruct((rows, 256), jnp.bfloat16),
        ),
        in_specs=[any_space] * 3,
        out_specs=(any_space,) * 3 + (vmem,) * 2,
        scratch_shapes=[
            pltpu.SemaphoreType.DMA((SLOTS,)),
            pltpu.SemaphoreType.DMA((SLOTS,)),
            pltpu.SemaphoreType.DMA((3,)),
            pltpu.VMEM((512, 768), jnp.float32),
            pltpu.VMEM((3, 32, 768), jnp.float32),
            pltpu.VMEM((32, 768), jnp.float32),
            pltpu.VMEM((32, 768), jnp.float32),
            pltpu.VMEM((2, 4, 2, 32, 768), jnp.float32),
            pltpu.VMEM((512, 512), jnp.float32),
            pltpu.VMEM((rows, 768), jnp.float32),
        ],
        compiler_params=pltpu.CompilerParams(
            collective_id=0, has_side_effects=True, vmem_limit_bytes=48 * 1024 * 1024
        ),
        name="exchange",
    )(eigenvectors, sets, gradient)


def update_kernel(coef_ref, x_ref, s_ref, g_ref, out_ref):
    across = (((1,), (1,)), ((), ()))
    update = lax.dot_general(
        coef_ref[:, :SPLIT], s_ref[...], across, preferred_element_type=jnp.float32
    ) + lax.dot_general(
        coef_ref[:, SPLIT:], g_ref[...], across, preferred_element_type=jnp.float32
    )
    out_ref[...] = (x_ref[...].astype(jnp.float32) - update).astype(jnp.bfloat16)


def renew(coefficients, slab, sets, gradient):
    rows, order = slab.shape
    block = order // 16
    return pl.pallas_call(
        update_kernel,
        grid=(16,),
        out_shape=jax.ShapeDtypeStruct(slab.shape, jnp.bfloat16),
        in_specs=[
            pl.BlockSpec(coefficients.shape, lambda i: (0, 0)),
            pl.BlockSpec((rows, block), lambda i: (0, i)),
            pl.BlockSpec((block, SPLIT), lambda i: (i, 0)),
            pl.BlockSpec((block, UPPER), lambda i: (i, 0)),
        ],
        out_specs=pl.BlockSpec((rows, block), lambda i: (0, i)),
        compiler_params=pltpu.CompilerParams(vmem_limit_bytes=32 * 1024 * 1024),
        name="renew",
    )(coefficients, slab, sets, gradient)


def body(eigenvectors, reflectors_first, reflectors_second, forget_gradient):
    sets = jnp.concatenate([reflectors_first, reflectors_second[:, :UPPER]], axis=1)
    rest = jnp.concatenate([reflectors_second[:, UPPER:], forget_gradient.T], axis=1)
    slab, all_sets, all_rest, coefficients, rotated = exchange(eigenvectors, sets, rest)
    renewed = renew(
        coefficients, slab, all_sets.reshape(-1, SPLIT), all_rest.reshape(-1, rest.shape[1])
    )
    return (renewed, rotated)


def solution(mesh):
    return jax.shard_map(
        body,
        mesh=mesh,
        in_specs=(
            P("col", "row"),
            P(("row", "col"), None),
            P(("row", "col"), None),
            P(None, ("row", "col")),
        ),
        out_specs=(P(("col", "row"), None), P(("col", "row"), None)),
        check_vma=False,
    )
```

time: 490 us -> 305 us (0.62)
  Pallas kernels: 10.7 us -> 292 us
  waiting for transfers between devices: 221 us -> 0 us
  blocking collectives: 181 us -> 0 us
  matrix products: 51.9 us -> 0 us
  between operations: 15.5 us -> 0.65 us
    pallas_call x1 -> x2, Pallas kernels: 10.7 us -> 292 us  [the longest x1 269 us: exchange(): pl.pallas_call(exchange_kernel, out_shape=(jax.ShapeDtypeStruct((rows, 8...]
    all_to_all x1 -> x0, blocking collectives: 181 us -> none  [body(): lax.all_to_all(renewed, 'row', split_axis=0, concat_axis=1, tiled=True)]
    psum x1 -> x0, waiting for transfers between devices: 126 us -> none  [body(): products = lax.psum(products, 'row')]
    all_gather x2 -> x0, waiting for transfers between devices: 94.7 us -> none  [the longest x1 58.8 us: body(): both_sets = lax.all_gather(own_sets, 'col', axis=0, tiled=True)]
    dot_general x5 -> x0, matrix products: 51.9 us -> none  [the longest x1 12.9 us: body(): lax.dot_general(eig_slab, lax.all_gather(forget_gradient, ('row', 'col'),...]
    all_to_all x1 -> x0, local copies, waits for them, and re-layouts: 5.5 us -> none  [body(): lax.all_to_all(renewed, 'row', split_axis=0, concat_axis=1, tiled=True)]
  transfers between devices with their start and end apart: 3 -> 0, of which waited for: 3 -> 0; matrix products, arithmetic and copies ran while one was open for 5% -> 0% of each run, Pallas kernels for 2% -> 0%
where the time goes in v3:
time: 305 us; the launch traced here: 300 us
  Pallas kernels  292 us (96%)
  local copies, waits for them, and re-layouts  6.15 us (2%)
    pallas_call x1, Pallas kernels, exchange(): pl.pallas_call(exchange_kernel, out_shape=(jax.ShapeDtypeStruct((rows, 8...  269 us
    pallas_call x1, Pallas kernels, renew(): pl.pallas_call(update_kernel, grid=(16,), out_shape=jax.ShapeDtypeStruct(...  23 us

profile of v3, /device:TPU:0, one launch (start us, length us, event | category | flops | bytes accessed | tf_op | source)
XLA Modules:
  0.0 299.6 jit_solution(8899898991933061988)
XLA Ops:
  0.6 0.9 fusion
  1.5 1.0 pad_maximum_fusion
  2.5 268.9 %exchange.1 = (bf16[224,28672]{1,0:T(8,128)(2,1)}, bf16[2,4,4,2,2,224,384]{6,5,4,3,2,1,0:T(8,128)(2,1)}, bf16[2,4,4,2,2,224,384]{6,5,4,3,2,1,0:T(8,128)(2,1)}, b...) custom-call(bf16[1792,3584]{1,0:T(8,128)(2,1)} %e_ref.1, bf16[224,384]{1,0:T(8,128)(2,1)S(1)} %get-tuple-element.14.s_ref, ...), custom_call_target="tpu_custom_call" | custom-call | tf_op jit(solution)/shard_map/exchange/pallas_call | solution.py:278
  271.4 0.0 copy-start
  271.4 4.6 %copy-done = bf16[224,28672]{1,0:T(8,128)(2,1)S(1)} copy-done((bf16[224,28672]{1,0:T(8,128)(2,1)S(1)}, bf16[224,28672]{1,0:T(8,128)(2,1)}, u32[]{:S(2)}) %copy-start) | copy-done | bytes 12845080
  276.0 23.0 %renew.1 = bf16[224,28672]{1,0:T(8,128)(2,1)} custom-call(bf16[224,512]{1,0:T(8,128)(2,1)S(1)} %get-tuple-element.7.coef_ref, bf16[224,28672]{1,0:T(8,128)(2,1)S(1)} %copy-done, bf16[28672,384]{1,0:T(8,128)(2,1)} %bitcast.3, bf16[28672,384]{1,0:T(8,128)(2,1)} %bitcast.4), custom_call_target="tpu_custom_call" | custom-call | tf_op jit(solution)/shard_map/renew/pallas_call | solution.py:321
  299.0 0.6 copy.7
Async XLA Ops:
  271.4 4.7 %copy-start = (bf16[224,28672]{1,0:T(8,128)(2,1)S(1)}, bf16[224,28672]{1,0:T(8,128)(2,1)}, u32[]{:S(2)}) copy-start(bf16[224,28672]{1,0:T(8,128)(2,1)} %get-tuple-element.8.x_ref) | copy-start | bytes 38535172

commit v4 on v3

--- a/solution.py
+++ b/solution.py
@@ -9,8 +9,7 @@
 HIGH = lax.Precision.HIGHEST
 BATCHES = 7
 SLOTS = 160
-SPLIT = 384
-UPPER = 128
+SPLIT = 512
 
 
 def exact(left_side, right_side):
@@ -133,9 +132,8 @@
         def step(s_block, g_block):
             s_value = s_block[...].reshape(-1, SPLIT)
             g_value = g_block[...].reshape(-1, g_block.shape[-1])
-            sets = jnp.concatenate([s_value, g_value[:, :UPPER]], axis=1)
-            part[:, :SPLIT] += inner_products(sets, s_value)
-            part[:, SPLIT:] += inner_products(sets, g_value)
+            part[:, :SPLIT] += inner_products(s_value, s_value)
+            part[:, SPLIT:] += inner_products(s_value, g_value)
 
         def spec(ref):
             return pl.BlockSpec(
@@ -144,49 +142,48 @@
 
         pltpu.emit_pipeline(step, grid=(8,), in_specs=[spec(sf_ref), spec(gf_ref)])(sf_ref, gf_ref)
 
-    def add_products(y_block, low, high):
+    def add_products(y_block):
         def step(x_block, s_block, g_block):
             x_value = x_block[...]
             s_value = s_block[...].reshape(-1, SPLIT)
             g_value = g_block[...].reshape(-1, g_block.shape[-1])
-            total[low:high, :SPLIT] += jnp.dot(x_value, s_value, preferred_element_type=jnp.float32)
-            total[low:high, SPLIT:] += jnp.dot(x_value, g_value, preferred_element_type=jnp.float32)
+            total[:, :SPLIT] += jnp.dot(x_value, s_value, preferred_element_type=jnp.float32)
+            total[:, SPLIT:] += jnp.dot(x_value, g_value, preferred_element_type=jnp.float32)
 
         def spec(ref):
             return pl.BlockSpec(
                 (None, None, None, 2, 2) + ref.shape[5:], lambda i: (i // 4, i % 4, y_block, 0, 0, 0, 0)
             )
 
-        x_rows = x_ref.at[pl.ds(low, high - low)]
-        x_spec = pl.BlockSpec((high - low, width // 4), lambda i: (0, i * 4 + y_block))
+        x_spec = pl.BlockSpec((rows, width // 4), lambda i: (0, i * 4 + y_block))
         pltpu.emit_pipeline(step, grid=(8,), in_specs=[x_spec, spec(sf_ref), spec(gf_ref)])(
-            x_rows, sf_ref, gf_ref)
+            x_ref, sf_ref, gf_ref)
 
     mine_s.start()
     mine_g.start()
     own, other = (zl, x, y, zh, k), (1 - zl, x, y, zh, k)
+    b1 = [t.start(g_ref, gf_ref.at[own], to) for to in near_x]
     a1 = t.start(s_ref, sf_ref.at[own], other_z)
-    a2a = [t.start(s_ref, sf_ref.at[own], to) for to in near_x]
-    b1 = [t.start(g_ref, gf_ref.at[own], to) for to in near_x]
+    a2 = [t.start(s_ref, sf_ref.at[own], to) for to in near_x]
     home = [t.start(s_ref, sf_ref.at[own], sib), t.start(g_ref, gf_ref.at[own], sib)]
     batch()
     mine.start()
     total[...] = jnp.zeros_like(total)
     mine_s.wait()
     mine_g.wait()
-    t.received(a1)
-    a2b = [push(sf_ref, other, to) for to in near_x]
-    t.received(*a2a)
-    a3 = [push(sf_ref, (zl, full, y, zh, k), cross)]
-    a4a = [[push(sf_ref, (zl, full, y, zh, k), near_y[d]) for d in (1, 3)]]
     t.received(*b1)
     b2 = push(gf_ref, (zl, full, y, zh, k), other_z)
-    t.received(*a2b)
+    t.received(a1)
+    a2_other = [push(sf_ref, other, to) for to in near_x]
+    t.received(b2)
+    b4 = {0: push(gf_ref, (full, full, y, zh, k), cross)}
+    b3 = {d: push(gf_ref, (full, full, y, zh, k), near_y[d]) for d in (1, 3)}
+    t.received(*a2)
+    a3 = [push(sf_ref, (zl, full, y, zh, k), cross)]
+    a4 = [[push(sf_ref, (zl, full, y, zh, k), near_y[d]) for d in (1, 3)]]
+    t.received(*a2_other)
     a3.append(push(sf_ref, (1 - zl, full, y, zh, k), cross))
-    a4a.append([push(sf_ref, (1 - zl, full, y, zh, k), near_y[d]) for d in (1, 3)])
-    t.received(b2)
-    b3 = {d: push(gf_ref, (full, full, y, zh, k), near_y[d]) for d in (1, 3, 2)}
-    b4 = {0: push(gf_ref, (full, full, y, zh, k), cross)}
+    a4.append([push(sf_ref, (1 - zl, full, y, zh, k), near_y[d]) for d in (1, 3)])
     home += [share(ref, other) for ref in (sf_ref, gf_ref)]
     home += [share(ref, (full, lax.rem(x + d, 4), y, zh, k)) for d in (1, 2, 3) for ref in (sf_ref, gf_ref)]
     batch()
@@ -194,76 +191,71 @@
     group_sums()
     slice_rows = pl.ds(pl.multiple_of((me * 2 + k) * 32, 32), 32)
     y_parts = [t.start(part.at[slice_rows], from_y.at[d - 1], near_y[d]) for d in (1, 2, 3)]
-
-    t.received(a3[0])
-    a4b = [[push(sf_ref, (1 - zl, full, y, 1 - zh, k), near_y[d]) for d in (1, 3)]]
-    t.received(a3[1])
-    a4b.append([push(sf_ref, (zl, full, y, 1 - zh, k), near_y[d]) for d in (1, 3)])
-    ready = {0: [share(sf_ref, (full, full, y, 1 - zh, k))]}
     batch()
     t.received(*y_parts)
     y_sum[...] = part[slice_rows, :] + from_y[0] + from_y[1] + from_y[2]
     z_part = t.start(y_sum, from_z, flip)
-
-    source = {1: lax.rem(y + 3, 4), 3: lax.rem(y + 1, 4), 2: lax.rem(y + 2, 4)}
-    far_own, far_other = [], []
-    for half, a in ((0, zl), (1, 1 - zl)):
-        t.received(a4a[half][0])
-        far_own.append(push(sf_ref, (a, full, source[1], zh, k), near_y[1]))
     t.received(z_part)
     sums[zl, x, k] = y_sum[...] + from_z[...]
     x_sums = [push(sums, (zl, x, k), to) for to in near_x]
+    t.received(*x_sums)
+    z_sums = push(sums, (zl, full, k), other_z)
+    for _ in range(BATCHES - len(batches)):
+        batch()
+    t.received(a3[0])
+    a5 = [[push(sf_ref, (1 - zl, full, y, 1 - zh, k), near_y[d]) for d in (1, 3)]]
+    t.received(a3[1])
+    a5.append([push(sf_ref, (zl, full, y, 1 - zh, k), near_y[d]) for d in (1, 3)])
+    ready = {0: [share(sf_ref, (full, full, y, 1 - zh, k))]}
+    t.received(z_sums)
+    sib_sums = push(sums, (full, full, k), sib)
+    rest_far = []
+    source = {1: lax.rem(y + 3, 4), 3: lax.rem(y + 1, 4), 2: lax.rem(y + 2, 4)}
     for d in (1, 3):
         t.received(b3[d])
         b4[d] = push(gf_ref, (full, full, source[d], zh, k), cross)
-        ready[d] = [b4[d], share(gf_ref, (full, full, source[d], zh, k))]
-    t.received(a4a[0][1], a4a[1][1])
+        ready[d] = [share(gf_ref, (full, full, source[d], zh, k))]
+        rest_far.append(push(gf_ref, (d // 2, full, source[d], zh, k), near_y[d]))
+    t.received(b4[0])
+    ready[0].append(share(gf_ref, (full, full, y, 1 - zh, k)))
+    far_own, far_other = [], []
+    for half, a in ((0, zl), (1, 1 - zl)):
+        t.received(a4[half][0])
+        far_own.append(push(sf_ref, (a, full, source[1], zh, k), near_y[1]))
+    t.received(*rest_far)
+    b4[2] = push(gf_ref, (full, full, source[2], zh, k), cross)
+    share(gf_ref, (full, full, source[2], zh, k))
+    t.received(a4[0][1], a4[1][1])
     for d in (1, 3):
         ready[d].append(share(sf_ref, (full, full, source[d], zh, k)))
-    batch()
-    t.received(*x_sums)
-    z_sums = push(sums, (zl, full, k), other_z)
-    t.received(b3[2])
-    b4[2] = push(gf_ref, (full, full, source[2], zh, k), cross)
-    ready[2] = [b4[2], share(gf_ref, (full, full, source[2], zh, k))]
-    batch()
-    t.received(z_sums)
-    sib_sums = push(sums, (full, full, k), sib)
-    t.received(b4[0])
-    ready[0].append(share(gf_ref, (full, full, y, 1 - zh, k)))
-    batch()
+    for half, a in ((0, 1 - zl), (1, zl)):
+        t.received(a5[half][1])
+        far_other.append(push(sf_ref, (a, full, source[3], 1 - zh, k), near_y[3]))
+    t.received(a5[0][0], a5[1][0])
+    for d in (1, 3):
+        ready[d].append(share(sf_ref, (full, full, source[d], 1 - zh, k)))
     t.received(sib_sums)
     invert_upper(sums[...].reshape(512, 768)[:, :512], inverse)
-    for half, a in ((0, 1 - zl), (1, zl)):
-        t.received(a4b[half][1])
-        far_other.append(push(sf_ref, (a, full, source[3], 1 - zh, k), near_y[3]))
-    t.received(a4b[0][0], a4b[1][0])
-    for d in (1, 3):
-        ready[d].append(share(sf_ref, (full, full, source[d], 1 - zh, k)))
-    batch()
-    mine.wait()
-    for slots in batches[:4]:
-        t.received(*slots)
-    t.received(*ready[0])
-    add_products(y, 0, 4 * piece)
-    t.received(*far_own)
-    ready[2].append(share(sf_ref, (full, full, source[2], zh, k)))
     for d in (1, 3):
         t.received(b4[d])
         ready[d].append(share(gf_ref, (full, full, source[d], 1 - zh, k)))
-    for d in (1, 3):
-        t.received(*ready[d])
-        add_products(source[d], 0, 4 * piece)
+    t.received(*far_own)
+    share(sf_ref, (full, full, source[2], zh, k))
+    mine.wait()
+    for slots in batches:
+        t.received(*slots)
+    t.received(*ready[0])
+    add_products(y)
+    t.received(*ready[1])
+    add_products(source[1])
     t.received(b4[2])
-    ready[2].append(share(gf_ref, (full, full, source[2], 1 - zh, k)))
+    share(gf_ref, (full, full, source[2], 1 - zh, k))
     t.received(*far_other)
-    ready[2].append(share(sf_ref, (full, full, source[2], 1 - zh, k)))
-    for slots in batches[4:]:
-        t.received(*slots)
-    for block in (y, source[1], source[3]):
-        add_products(block, 4 * piece, rows)
+    share(sf_ref, (full, full, source[2], 1 - zh, k))
+    t.received(*ready[3])
+    add_products(source[3])
     t.finish()
-    add_products(source[2], 0, rows)
+    add_products(source[2])
     coefficients = exact(total[:, :512], inverse[...]).astype(jnp.bfloat16)
     coef_ref[...] = coefficients
     changed = exact(coefficients.astype(jnp.float32), sums[...].reshape(512, 768)[:, 512:])
@@ -305,43 +297,14 @@
     )(eigenvectors, sets, gradient)
 
 
-def update_kernel(coef_ref, x_ref, s_ref, g_ref, out_ref):
-    across = (((1,), (1,)), ((), ()))
+def body(eigenvectors, reflectors_first, reflectors_second, forget_gradient):
+    sets = jnp.concatenate([reflectors_first, reflectors_second], axis=1)
+    slab, all_sets, _, coefficients, rotated = exchange(eigenvectors, sets, forget_gradient.T)
     update = lax.dot_general(
-        coef_ref[:, :SPLIT], s_ref[...], across, preferred_element_type=jnp.float32
-    ) + lax.dot_general(
-        coef_ref[:, SPLIT:], g_ref[...], across, preferred_element_type=jnp.float32
+        coefficients, all_sets.reshape(-1, sets.shape[1]), (((1,), (1,)), ((), ())),
+        preferred_element_type=jnp.float32,
     )
-    out_ref[...] = (x_ref[...].astype(jnp.float32) - update).astype(jnp.bfloat16)
-
-
-def renew(coefficients, slab, sets, gradient):
-    rows, order = slab.shape
-    block = order // 16
-    return pl.pallas_call(
-        update_kernel,
-        grid=(16,),
-        out_shape=jax.ShapeDtypeStruct(slab.shape, jnp.bfloat16),
-        in_specs=[
-            pl.BlockSpec(coefficients.shape, lambda i: (0, 0)),
-            pl.BlockSpec((rows, block), lambda i: (0, i)),
-            pl.BlockSpec((block, SPLIT), lambda i: (i, 0)),
-            pl.BlockSpec((block, UPPER), lambda i: (i, 0)),
-        ],
-        out_specs=pl.BlockSpec((rows, block), lambda i: (0, i)),
-        compiler_params=pltpu.CompilerParams(vmem_limit_bytes=32 * 1024 * 1024),
-        name="renew",
-    )(coefficients, slab, sets, gradient)
-
-
-def body(eigenvectors, reflectors_first, reflectors_second, forget_gradient):
-    sets = jnp.concatenate([reflectors_first, reflectors_second[:, :UPPER]], axis=1)
-    rest = jnp.concatenate([reflectors_second[:, UPPER:], forget_gradient.T], axis=1)
-    slab, all_sets, all_rest, coefficients, rotated = exchange(eigenvectors, sets, rest)
-    renewed = renew(
-        coefficients, slab, all_sets.reshape(-1, SPLIT), all_rest.reshape(-1, rest.shape[1])
-    )
-    return (renewed, rotated)
+    return ((slab.astype(jnp.float32) - update).astype(jnp.bfloat16), rotated)
 
 
 def solution(mesh):

time: 305 us -> 256 us (0.84); the launches traced: 300 us -> 255 us
  Pallas kernels: 292 us -> 232 us
  matrix products: 0 us -> 19.9 us
  local copies, waits for them, and re-layouts: 6.15 us -> 1.54 us
    pallas_call x1, Pallas kernels: 269 us -> 232 us  [exchange(): pl.pallas_call(exchange_kernel, out_shape=(jax.ShapeDtypeStruct((rows, 8...]
    pallas_call x1 -> x0, Pallas kernels: 23 us -> none  [renew(): pl.pallas_call(update_kernel, grid=(16,), out_shape=jax.ShapeDtypeStruct(...]
    dot_general x0 -> x1, matrix products: none -> 19.9 us  [body(): lax.dot_general(coefficients, all_sets.reshape(-1, sets.shape[1]), (((1,)...]
    unnamed x3, local copies, waits for them, and re-layouts: 5.29 us -> 1.54 us
where the time goes in v4:
time: 256 us; the launch traced here: 255 us
  Pallas kernels  232 us (91%)
  matrix products  19.9 us (8%)
    pallas_call x1, Pallas kernels, exchange(): pl.pallas_call(exchange_kernel, out_shape=(jax.ShapeDtypeStruct((rows, 8...  232 us
    dot_general x1, matrix products, body(): lax.dot_general(coefficients, all_sets.reshape(-1, sets.shape[1]), (((1,)...  19.9 us

profile of v4, /device:TPU:0, one launch (start us, length us, event | category | flops | bytes accessed | tf_op | source)
XLA Modules:
  0.0 254.7 jit_solution(13570515023117838554)
XLA Ops:
  0.6 1.0 pad_maximum_fusion.s_ref
  1.6 0.0 copy-start
  1.6 0.9 copy-done
  2.5 231.6 %exchange.1 = (bf16[224,28672]{1,0:T(8,128)(2,1)}, bf16[2,4,4,2,2,224,512]{6,5,4,3,2,1,0:T(8,128)(2,1)}, bf16[2,4,4,2,2,224,256]{6,5,4,3,2,1,0:T(8,128)(2,1)}, b...) custom-call(bf16[1792,3584]{1,0:T(8,128)(2,1)} %e_ref.1, bf16[224,512]{1,0:T(8,128)(2,1)S(1)} %pad_maximum_fusion.s_ref, ...), custom_call_target="tpu_custom_call" | custom-call | tf_op jit(solution)/shard_map/exchange/pallas_call | solution.py:270
  234.1 19.9 %fusion = bf16[224,28672]{1,0:T(8,128)(2,1)} fusion(bf16[224,512]{1,0:T(8,128)(2,1)S(1)} %get-tuple-element.7, bf16[28672,512]{1,0:T(8,128)(2,1)} %bitcast.5, bf16[224,28672]{1,0:T(8,128)(2,1)} %get-tuple-element.6), kind=kOutput, calls=%fused_computation.1 | convolution fusion | flops 6595936256 | bytes 55279616 | tf_op jit(solution)/shard_map/dot_general | solution.py:303
  254.0 0.6 copy.7
Async XLA Ops:
  1.6 0.9 copy-start

commit v5 on v4

--- a/solution.py
+++ b/solution.py
@@ -7,7 +7,7 @@
 
 MESH = pl.DeviceIdType.MESH
 HIGH = lax.Precision.HIGHEST
-BATCHES = 7
+BATCHES = 8
 SLOTS = 160
 SPLIT = 512
 
@@ -102,16 +102,22 @@
     t = Transfers(send_sem, recv_sem)
     rows, width = x_ref.shape[0], e_ref.shape[1]
     own_columns = pl.ds(pl.multiple_of(me * width, 128), width)
-    piece = rows // BATCHES
+    source = {1: lax.rem(y + 3, 4), 3: lax.rem(y + 1, 4), 2: lax.rem(y + 2, 4)}
+    y_order = [y, source[1], source[3], source[2]]
     batches = []
     full = slice(None)
 
     def batch():
         q = len(batches)
+        half, block = rows // 2, width // 4
+        low, offset = (q % 2) * half, y_order[q // 2] * block
         slots = []
         for to in partners:
-            source = e_ref.at[pl.ds(pl.multiple_of(to[0] * rows + q * piece, 16), piece)]
-            slots.append(t.start(source, x_ref.at[pl.ds(q * piece, piece), own_columns], to))
+            source_rows = pl.ds(pl.multiple_of(to[0] * rows + low, 16), half)
+            source_columns = pl.ds(pl.multiple_of(offset, 128), block)
+            target_columns = pl.ds(pl.multiple_of(me * width + offset, 128), block)
+            slots.append(t.start(
+                e_ref.at[source_rows, source_columns], x_ref.at[pl.ds(low, half), target_columns], to))
         batches.append(slots)
 
     def push(ref, index, to):
@@ -210,7 +216,6 @@
     t.received(z_sums)
     sib_sums = push(sums, (full, full, k), sib)
     rest_far = []
-    source = {1: lax.rem(y + 3, 4), 3: lax.rem(y + 1, 4), 2: lax.rem(y + 2, 4)}
     for d in (1, 3):
         t.received(b3[d])
         b4[d] = push(gf_ref, (full, full, source[d], zh, k), cross)
@@ -239,20 +244,18 @@
     for d in (1, 3):
         t.received(b4[d])
         ready[d].append(share(gf_ref, (full, full, source[d], 1 - zh, k)))
+    mine.wait()
+    t.received(*ready[0], *batches[0], *batches[1])
+    add_products(y)
     t.received(*far_own)
     share(sf_ref, (full, full, source[2], zh, k))
-    mine.wait()
-    for slots in batches:
-        t.received(*slots)
-    t.received(*ready[0])
-    add_products(y)
-    t.received(*ready[1])
+    t.received(*ready[1], *batches[2], *batches[3])
     add_products(source[1])
     t.received(b4[2])
     share(gf_ref, (full, full, source[2], 1 - zh, k))
     t.received(*far_other)
     share(sf_ref, (full, full, source[2], 1 - zh, k))
-    t.received(*ready[3])
+    t.received(*ready[3], *batches[4], *batches[5])
     add_products(source[3])
     t.finish()
     add_products(source[2])

time: 256 us -> 242 us (0.945)
  Pallas kernels: 232 us -> 219 us
    pallas_call x1, Pallas kernels: 232 us -> 219 us  [exchange(): pl.pallas_call(exchange_kernel, out_shape=(jax.ShapeDtypeStruct((rows, 8...]
where the time goes in v5:
time: 242 us
  Pallas kernels  219 us (90%)
  matrix products  19.9 us (8%)
    pallas_call x1, Pallas kernels, exchange(): pl.pallas_call(exchange_kernel, out_shape=(jax.ShapeDtypeStruct((rows, 8...  219 us
    dot_general x1, matrix products, body(): lax.dot_general(coefficients, all_sets.reshape(-1, sets.shape[1]), (((1,)...  19.9 us

profile of v5, /device:TPU:0, one launch (start us, length us, event | category | flops | bytes accessed | tf_op | source)
XLA Modules:
  0.0 241.6 jit_solution(2581784216915476725)
XLA Ops:
  0.6 1.0 pad_maximum_fusion.s_ref
  1.6 0.0 copy-start
  1.6 0.9 copy-done
  2.5 218.6 %exchange.1 = (bf16[224,28672]{1,0:T(8,128)(2,1)}, bf16[2,4,4,2,2,224,512]{6,5,4,3,2,1,0:T(8,128)(2,1)}, bf16[2,4,4,2,2,224,256]{6,5,4,3,2,1,0:T(8,128)(2,1)}, b...) custom-call(bf16[1792,3584]{1,0:T(8,128)(2,1)} %e_ref.1, bf16[224,512]{1,0:T(8,128)(2,1)S(1)} %pad_maximum_fusion.s_ref, ...), custom_call_target="tpu_custom_call" | custom-call | tf_op jit(solution)/shard_map/exchange/pallas_call | solution.py:273
  221.1 19.9 %fusion = bf16[224,28672]{1,0:T(8,128)(2,1)} fusion(bf16[224,512]{1,0:T(8,128)(2,1)S(1)} %get-tuple-element.7, bf16[28672,512]{1,0:T(8,128)(2,1)} %bitcast.5, bf16[224,28672]{1,0:T(8,128)(2,1)} %get-tuple-element.6), kind=kOutput, calls=%fused_computation.1 | convolution fusion | flops 6595936256 | bytes 55279616 | tf_op jit(solution)/shard_map/dot_general | solution.py:306
  241.0 0.6 copy.7
Async XLA Ops:
  1.6 0.9 copy-start

commit v6 on v5

--- a/solution.py
+++ b/solution.py
@@ -80,7 +80,7 @@
 
 
 def exchange_kernel(
-    e_ref, s_ref, g_ref, x_ref, sf_ref, gf_ref, coef_ref, rot_ref,
+    e_ref, s1_ref, s2_ref, g_ref, x_ref, sf_ref, gf_ref, coef_ref, rot_ref,
     send_sem, recv_sem, local_sem, part, from_y, y_sum, from_z, sums, inverse, total,
 ):
     zl, x, y, zh, k = place()
@@ -129,8 +129,11 @@
 
     mine = pltpu.make_async_copy(
         e_ref.at[pl.ds(pl.multiple_of(me * rows, 16), rows)], x_ref.at[:, own_columns], local_sem.at[0])
-    mine_s = pltpu.make_async_copy(s_ref, sf_ref.at[zl, x, y, zh, k], local_sem.at[1])
-    mine_g = pltpu.make_async_copy(g_ref, gf_ref.at[zl, x, y, zh, k], local_sem.at[2])
+    mine_s = [
+        pltpu.make_async_copy(
+            ref, sf_ref.at[zl, x, y, zh, k, :, pl.ds(i * ref.shape[1], ref.shape[1])], local_sem.at[1 + i])
+        for i, ref in enumerate((s1_ref, s2_ref))]
+    mine_g = pltpu.make_async_copy(g_ref, gf_ref.at[zl, x, y, zh, k], local_sem.at[3])
 
     def group_sums():
         part[...] = jnp.zeros_like(part)
@@ -165,22 +168,24 @@
         pltpu.emit_pipeline(step, grid=(8,), in_specs=[x_spec, spec(sf_ref), spec(gf_ref)])(
             x_ref, sf_ref, gf_ref)
 
-    mine_s.start()
+    for copy in mine_s:
+        copy.start()
     mine_g.start()
     own, other = (zl, x, y, zh, k), (1 - zl, x, y, zh, k)
     b1 = [t.start(g_ref, gf_ref.at[own], to) for to in near_x]
-    a1 = t.start(s_ref, sf_ref.at[own], other_z)
-    a2 = [t.start(s_ref, sf_ref.at[own], to) for to in near_x]
-    home = [t.start(s_ref, sf_ref.at[own], sib), t.start(g_ref, gf_ref.at[own], sib)]
-    batch()
+    for copy in mine_s:
+        copy.wait()
+    a1 = push(sf_ref, own, other_z)
+    a2 = [push(sf_ref, own, to) for to in near_x]
+    home = [push(sf_ref, own, sib), t.start(g_ref, gf_ref.at[own], sib)]
     mine.start()
     total[...] = jnp.zeros_like(total)
-    mine_s.wait()
     mine_g.wait()
     t.received(*b1)
     b2 = push(gf_ref, (zl, full, y, zh, k), other_z)
     t.received(a1)
     a2_other = [push(sf_ref, other, to) for to in near_x]
+    batch()
     t.received(b2)
     b4 = {0: push(gf_ref, (full, full, y, zh, k), cross)}
     b3 = {d: push(gf_ref, (full, full, y, zh, k), near_y[d]) for d in (1, 3)}
@@ -265,7 +270,7 @@
     rot_ref[...] = (total[:, 512:] - changed).astype(jnp.bfloat16)
 
 
-def exchange(eigenvectors, sets, gradient):
+def exchange(eigenvectors, first, second, gradient):
     blocks = (2, 4, 4, 2, 2)
     rows, width = eigenvectors.shape[0] // 8, eigenvectors.shape[1]
     any_space = pl.BlockSpec(memory_space=pl.ANY)
@@ -274,17 +279,17 @@
         exchange_kernel,
         out_shape=(
             jax.ShapeDtypeStruct((rows, 8 * width), jnp.bfloat16),
-            jax.ShapeDtypeStruct(blocks + sets.shape, jnp.bfloat16),
+            jax.ShapeDtypeStruct(blocks + (first.shape[0], SPLIT), jnp.bfloat16),
             jax.ShapeDtypeStruct(blocks + gradient.shape, jnp.bfloat16),
             jax.ShapeDtypeStruct((rows, 512), jnp.bfloat16),
             jax.ShapeDtypeStruct((rows, 256), jnp.bfloat16),
         ),
-        in_specs=[any_space] * 3,
+        in_specs=[any_space] * 4,
         out_specs=(any_space,) * 3 + (vmem,) * 2,
         scratch_shapes=[
             pltpu.SemaphoreType.DMA((SLOTS,)),
             pltpu.SemaphoreType.DMA((SLOTS,)),
-            pltpu.SemaphoreType.DMA((3,)),
+            pltpu.SemaphoreType.DMA((4,)),
             pltpu.VMEM((512, 768), jnp.float32),
             pltpu.VMEM((3, 32, 768), jnp.float32),
             pltpu.VMEM((32, 768), jnp.float32),
@@ -297,14 +302,15 @@
             collective_id=0, has_side_effects=True, vmem_limit_bytes=48 * 1024 * 1024
         ),
         name="exchange",
-    )(eigenvectors, sets, gradient)
+    )(eigenvectors, first, second, gradient)
 
 
 def body(eigenvectors, reflectors_first, reflectors_second, forget_gradient):
-    sets = jnp.concatenate([reflectors_first, reflectors_second], axis=1)
-    slab, all_sets, _, coefficients, rotated = exchange(eigenvectors, sets, forget_gradient.T)
+    slab, all_sets, _, coefficients, rotated = exchange(
+        eigenvectors, reflectors_first, reflectors_second, forget_gradient.T
+    )
     update = lax.dot_general(
-        coefficients, all_sets.reshape(-1, sets.shape[1]), (((1,), (1,)), ((), ())),
+        coefficients, all_sets.reshape(-1, SPLIT), (((1,), (1,)), ((), ())),
         preferred_element_type=jnp.float32,
     )
     return ((slab.astype(jnp.float32) - update).astype(jnp.bfloat16), rotated)

time: 242 us -> 241 us (level); the launches traced: 242 us -> 238 us
  Pallas kernels: 219 us -> 214 us
    pallas_call x1, Pallas kernels: 219 us -> 214 us  [exchange(): pl.pallas_call(exchange_kernel, out_shape=(jax.ShapeDtypeStruct((rows, 8...]
where the time goes in v6:
time: 241 us; the launch traced here: 238 us
  Pallas kernels  214 us (89%)
  matrix products  19.9 us (8%)
  local copies, waits for them, and re-layouts  3.33 us (1%)
    pallas_call x1, Pallas kernels, exchange(): pl.pallas_call(exchange_kernel, out_shape=(jax.ShapeDtypeStruct((rows, 8...  214 us
    dot_general x1, matrix products, body(): lax.dot_general(coefficients, all_sets.reshape(-1, SPLIT), (((1,), (1,)),...  19.9 us

profile of v6, /device:TPU:0, one launch (start us, length us, event | category | flops | bytes accessed | tf_op | source)
XLA Modules:
  0.0 238.2 jit_solution(1713155044900636940)
XLA Ops:
  0.6 0.0 copy-start
  0.6 0.9 copy-done
  1.5 0.0 copy-start.1
  1.5 0.9 copy-done.1
  2.4 0.0 copy-start.2
  2.4 0.9 copy-done.2
  3.3 214.3 %exchange.1 = (bf16[224,28672]{1,0:T(8,128)(2,1)}, bf16[2,4,4,2,2,224,512]{6,5,4,3,2,1,0:T(8,128)(2,1)}, bf16[2,4,4,2,2,224,256]{6,5,4,3,2,1,0:T(8,128)(2,1)}, b...) custom-call(bf16[1792,3584]{1,0:T(8,128)(2,1)} %e_ref.1, bf16[224,256]{1,0:T(8,128)(2,1)S(1)} %copy-done, ...), custom_call_target="tpu_custom_call" | custom-call | tf_op jit(solution)/shard_map/exchange/pallas_call | solution.py:278
  217.7 19.9 %fusion = bf16[224,28672]{1,0:T(8,128)(2,1)} fusion(bf16[224,512]{1,0:T(8,128)(2,1)S(1)} %get-tuple-element.7, bf16[28672,512]{1,0:T(8,128)(2,1)} %bitcast.5, bf16[224,28672]{1,0:T(8,128)(2,1)} %get-tuple-element.6), kind=kOutput, calls=%fused_computation.1 | convolution fusion | flops 6595936256 | bytes 55279616 | tf_op jit(solution)/shard_map/dot_general | solution.py:312
  237.5 0.6 copy.7
Async XLA Ops:
  0.6 0.9 copy-start
  1.5 0.9 copy-start.1
  2.4 0.9 copy-start.2
